TPU v7x, 32 devices: a whole 2x2x4 slice. The times are simulated.
32 devices in a mesh: parts: 2 (over y), wide: 8 (over z, x), tp: 2 (over core).
Axes of the slice: x: 2, y: 2, z: 4, core: 2. Of those that a mesh axis runs over, the one named last changes fastest.
Arguments:
- queries: bfloat16 [16, 3, 8192], P(('parts', 'wide'), None, 'tp'), parts along dimension 0, may hold values from -6 to 6
- cache_kv: bfloat16 [2, 32, 1024, 1024], P(None, ('parts', 'wide'), None, 'tp'), parts along dimension 1, may hold values from -6 to 6
- fresh_kv: bfloat16 [2, 16, 3, 1024], P(None, ('parts', 'wide'), None, 'tp'), parts along dimension 1, may hold values from -6 to 6
- ctx_len: int32 [32], P(('parts', 'wide')), parts along dimension 0, may hold values from 1 to 1024, 8711 in all
- prefill: bfloat16 [2, 16, 2048, 1024], P(None, ('parts', 'wide'), None, 'tp'), parts along dimension 1, may hold values from -6 to 6
- prefill_scale: bfloat16 [2, 16, 2048, 8], P(None, ('parts', 'wide'), None, 'tp'), parts along dimension 1, may hold values from 0.25 to 4
- new_group: int32 [16], P('parts'), parts along dimension 0, may hold values from 0 to 7, as said below
- new_pages: int32 [16], P('parts'), parts along dimension 0, may hold values from 1 to 128, 579 in all
Outputs:
- attended: bfloat16 [16, 3, 8192], P(('parts', 'wide'), None, 'tp'), parts along dimension 0
- handed_kv: bfloat16 [2, 16, 1, 2048, 1024], P(None, ('parts', 'wide'), None, None, 'tp'), parts along dimension 1
There are 2 independent parts, one for each index of `parts`. A program takes and returns all parts, laid end to end along the dimension named above; each array names one. Nothing has to cross between parts.
Inputs may be any that keep to these rules, and one draw needn't show every extreme that they name: `new_group`: every decode group receives exactly 1 new requests. `ctx_len`: cached positions of a resident request; at least one. A new request's prompt has new_pages * 16 positions; the rest of its rows in prefill are unused.
All inputs are finite; a program needn't handle non-finite values. No bound on the sum of `ctx_len` on one device may be relied on, other than what follows from the above.
Results may differ from a plain program's by a relative error of at most 0.008.
Values may be sent and summed in bfloat16 or wider, within the bound.
A program may use at most 128 MiB of HBM per device.

v0:
```python
import math

import jax
import jax.numpy as jnp
from jax import lax
from jax.sharding import PartitionSpec as P

HD = 128
PAGE = 16


NEG_FILL = -1e30


def group_ranks(groups):
    request_ids = jnp.arange(groups.shape[0], dtype=jnp.int32)
    earlier = (groups[None, :] == groups[:, None]) & (request_ids[None, :] < request_ids[:, None])
    return jnp.sum(earlier.astype(jnp.int32), axis=1)


def dequantize(values, scales):
    full_shape = values.shape
    widened = values.astype(jnp.float32).reshape(
        full_shape[:-1] + (scales.shape[-1], full_shape[-1] // scales.shape[-1])
    )
    return (
        (widened * scales.astype(jnp.float32)[..., None]).reshape(full_shape).astype(jnp.bfloat16)
    )


def self_score(asked_rows, fresh_key):
    rows_count = asked_rows.shape[0]
    heads_kv = fresh_key.shape[-1] // HD
    grouped = asked_rows.reshape(rows_count, heads_kv, -1, HD)
    own_key = fresh_key.reshape(rows_count, heads_kv, HD)
    return jnp.einsum("rgjd,rgd->rgj", grouped, own_key, preferred_element_type=jnp.float32) * (
        1.0 / math.sqrt(HD)
    )


def masked_scores(asked_rows, key_rows, usable):
    rows_count, span_len, width_all = key_rows.shape
    heads_kv = width_all // HD
    grouped = asked_rows.reshape(rows_count, heads_kv, -1, HD)
    keyed = key_rows.reshape(rows_count, span_len, heads_kv, HD)
    scores = jnp.einsum("rgjd,rlgd->rgjl", grouped, keyed, preferred_element_type=jnp.float32) * (
        1.0 / math.sqrt(HD)
    )
    return jnp.where(usable[:, None, None, :], scores, NEG_FILL)


def weighted_sum(weights, value_rows):
    rows_count, span_len, width_all = value_rows.shape
    valued = value_rows.reshape(rows_count, span_len, width_all // HD, HD)
    return jnp.einsum(
        "rgjl,rlgd->rgjd", weights.astype(jnp.bfloat16), valued, preferred_element_type=jnp.float32
    )


def own_term(own_weight, fresh_value):
    rows_count = fresh_value.shape[0]
    own_rounded = lax.optimization_barrier(own_weight.astype(jnp.bfloat16)).astype(jnp.float32)
    own_value = fresh_value.astype(jnp.float32).reshape(
        rows_count, fresh_value.shape[-1] // HD, 1, HD
    )
    return own_rounded[..., None] * own_value


def attend(asked_rows, key_rows, value_rows, lengths, fresh_key, fresh_value):
    rows_count = asked_rows.shape[0]
    usable = jnp.arange(key_rows.shape[1], dtype=jnp.int32)[None, :] < lengths[:, None]
    scores = masked_scores(asked_rows, key_rows, usable)
    own_score = self_score(asked_rows, fresh_key)
    peak = jnp.maximum(jnp.max(scores, axis=-1), own_score)
    weights = jnp.where(usable[:, None, None, :], jnp.exp(scores - peak[..., None]), 0.0)
    own_weight = jnp.exp(own_score - peak)
    total = jnp.sum(weights, axis=-1) + own_weight
    summed = weighted_sum(weights, value_rows) + own_term(own_weight, fresh_value)
    return (summed / total[..., None]).reshape(rows_count, -1).astype(jnp.bfloat16)


def on_device(queries, cache_kv, fresh_kv, ctx_len, prefill, prefill_scale, new_group, new_pages):
    groups_count = lax.axis_size("wide")
    device_index = lax.axis_index("wide")
    new_total = new_group.shape[0]
    per_group = new_total // groups_count
    resident_count = cache_kv.shape[1]
    prompt_len = prefill.shape[2]
    piece_len = prompt_len // groups_count
    width_here = prefill.shape[3]
    slot_ids = new_group * per_group + group_ranks(new_group)
    arrival = (
        jnp.zeros((new_total,), jnp.int32).at[slot_ids].set(jnp.arange(new_total, dtype=jnp.int32))
    )
    new_len = new_pages * PAGE
    first_slot = device_index * per_group
    slot_len = lax.dynamic_slice_in_dim(new_len[arrival], first_slot, per_group)
    positions = jnp.arange(prompt_len, dtype=jnp.int32)
    asked_rows = queries[0]
    own_fresh = fresh_kv[:, 0]
    older_rows = attend(
        asked_rows[:resident_count],
        cache_kv[0],
        cache_kv[1],
        ctx_len,
        own_fresh[0, :resident_count],
        own_fresh[1, :resident_count],
    )
    own_len = lax.dynamic_slice_in_dim(new_len, first_slot, per_group)
    local_kv = dequantize(prefill, prefill_scale)
    keeping = positions[None, :] < own_len[:, None]
    local_kv = jnp.where(keeping[None, :, :, None], local_kv, jnp.zeros((), jnp.bfloat16))
    split_kv = local_kv.reshape(2, per_group, groups_count, piece_len, width_here)
    held = lax.all_to_all(split_kv, "wide", split_axis=2, concat_axis=1, tiled=True)
    ordered = held[:, arrival]
    handed = lax.all_to_all(ordered, "wide", split_axis=1, concat_axis=3, tiled=True)
    newer_rows = attend(
        asked_rows[resident_count:],
        handed[0, 0],
        handed[1, 0],
        slot_len,
        own_fresh[0, resident_count:],
        own_fresh[1, resident_count:],
    )
    attended = jnp.concatenate([older_rows, newer_rows], axis=0)[None]
    return (attended, handed)


def solution(mesh):
    return jax.shard_map(
        on_device,
        mesh=mesh,
        in_specs=(
            P(("parts", "wide"), None, "tp"),
            P(None, ("parts", "wide"), None, "tp"),
            P(None, ("parts", "wide"), None, "tp"),
            P(("parts", "wide")),
            P(None, ("parts", "wide"), None, "tp"),
            P(None, ("parts", "wide"), None, "tp"),
            P("parts"),
            P("parts"),
        ),
        out_specs=(P(("parts", "wide"), None, "tp"), P(None, ("parts", "wide"), None, None, "tp")),
        check_vma=False,
    )
```

profile of v0, /device:TPU:0, one launch (start us, length us, event | category | flops | bytes accessed | tf_op | source)
XLA Modules:
  0.0 253.0 jit_solution(17578923951197465894)
XLA Ops:
  0.6 0.8 bitcast_convert_fusion
  1.4 0.6 copy.64
  2.0 6.1 %mul.89 = f32[2,2048,4,128]{3,2,1,0:T(4,128)} broadcast(f32[2,2048,4]{2,1,0:T(8,128)S(1)} %copy.64), dimensions={0,1,2} | broadcast | bytes 8454144 | tf_op jit(solution)/shard_map/mul | solution.py:27
  8.1 0.0 copy-start.4
  8.1 10.3 %mul.90 = f32[2,1,2048,512]{3,2,0,1:T(8,128)} reshape(f32[2,2048,4,128]{3,2,1,0:T(4,128)} %mul.89) | data formatting | bytes 16777216 | tf_op jit(solution)/shard_map/mul | solution.py:27
  18.4 0.0 copy-done.4
  18.4 0.6 dynamic_slice.7
  19.0 0.7 iota_compare_fusion
  19.7 5.2 %fusion = bf16[2,1,2048,512]{3,2,0,1:T(8,128)(2,1)S(1)} fusion(f32[2,1,2048,512]{3,2,0,1:T(8,128)} %mul.90, bf16[2,1,2048,512]{3,2,1,0:T(8,128)(2,1)} %param.12, pred[2048]{0:T(1024)(128)(4,1)S(1)} %iota_compare_fusion), kind=kLoop, calls=%fused_computation.4 | loop fusion | flops 8388608 | bytes 16779264 | tf_op jit(solution)/shard_map/jit(_where)/select_n | solution.py:112
  24.9 2.4 copy.65
  27.4 0.0 copy-start.5
  27.4 7.4 %all-to-all-start = ((bf16[2,1,8,256,512]{4,3,0,1,2:T(8,128)(2,1)}), bf16[2,1,8,256,512]{4,3,0,1,2:T(8,128)(2,1)}, u32[]{:S(2)}, u32[]{:S(2)}) async-start(bf16[2,1,8,256,512]{4,3,0,1,2:T(8,128)(2,1)} %copy.65), calls=%async_computation | async-start | bytes 8388608 | tf_op jit(solution)/shard_map/all_to_all | solution.py:114
  34.7 0.0 copy-done.5
  34.8 0.2 convert_reduce_fusion
  35.0 0.6 scatter_custom_fusion
  35.6 92.5 %all-to-all-done = bf16[2,1,8,256,512]{4,3,0,1,2:T(8,128)(2,1)} async-done(((bf16[2,1,8,256,512]{4,3,0,1,2:T(8,128)(2,1)}), bf16[2,1,8,256,512]{4,3,0,1,2:T(8,128)(2,1)}, u32[]{:S(2)}, u32[]{:S(2)}) %all-to-all-start) | async-done | bytes 4194336 | tf_op jit(solution)/shard_map/all_to_all | solution.py:114
  128.0 4.6 %copy.116 = bf16[2,1,8,256,512]{4,3,2,0,1:T(8,128)(2,1)} copy(bf16[2,1,8,256,512]{4,3,0,1,2:T(8,128)(2,1)} %all-to-all-done) | data formatting | bytes 8388608 | tf_op jit(solution)/shard_map/all_to_all | solution.py:114
  132.6 5.0 %gather_fusion.1 = bf16[8,2,256,512]{3,2,1,0:T(8,128)(2,1)} fusion(bf16[2,8,256,512]{3,2,1,0:T(8,128)(2,1)} %bitcast.79, s32[1024]{0:T(1024)S(1)} %pad_clamp_fusion), kind=kCustom, calls=%fused_computation.1 | custom fusion | bytes 8388640 | tf_op jit(solution)/shard_map/gather | solution.py:115
  137.6 4.5 %all-to-all-start.1 = ((bf16[2,8,1,256,512]{4,3,0,2,1:T(8,128)(2,1)}), bf16[2,8,1,256,512]{4,3,0,2,1:T(8,128)(2,1)}, u32[]{:S(2)}, u32[]{:S(2)}) async-start(bf16[2,8,1,256,512]{4,3,0,2,1:T(8,128)(2,1)} %bitcast.78), calls=%async_computation.1 | async-start | bytes 8388608 | tf_op jit(solution)/shard_map/all_to_all | solution.py:116
  142.1 0.6 gather_fusion
  142.8 0.6 dynamic_slice.6
  143.4 4.6 %fusion.47 = (bf16[1,2,1024,512]{3,2,1,0:T(8,128)(2,1)}, bf16[1,2,1024,512]{3,2,1,0:T(8,128)(2,1)}) fusion(bf16[2,2,1024,512]{3,2,1,0:T(8,128)(2,1)} %param.9), kind=kLoop, calls=%fused_computation.73 | loop fusion | bytes 8388608 | tf_op jit(solution)/shard_map/slice | solution.py:103
  147.9 3.0 %copy.89 = bf16[1,2,1024,512]{2,3,1,0:T(8,128)(2,1)S(1)} copy(bf16[1,2,1024,512]{3,2,1,0:T(8,128)(2,1)} %get-tuple-element.11) | data formatting | bytes 4194304
  150.9 0.0 copy-start.3
  150.9 0.0 copy-start.1
  151.0 0.0 copy-start.2
  151.0 4.0 %copy.88 = bf16[1,2,1024,512]{2,3,1,0:T(8,128)(2,1)} copy(bf16[1,2,1024,512]{3,2,1,0:T(8,128)(2,1)} %get-tuple-element.10) | data formatting | bytes 4194304
  154.9 0.0 copy-done.3
  154.9 0.1 iota_compare_fusion.2
  155.0 0.0 copy-done.1
  155.0 0.0 copy-done.2
  155.0 0.1 fusion.31
  155.2 2.1 fusion.50
  157.2 0.2 fusion.19
  157.5 0.7 fusion.15
  158.2 0.7 iota_compare_fusion.1
  158.9 0.1 slice_reduce_fusion
  158.9 0.1 fusion.36
  159.1 75.6 %all-to-all-done.1 = bf16[2,8,1,256,512]{4,3,0,2,1:T(8,128)(2,1)} async-done(((bf16[2,8,1,256,512]{4,3,0,2,1:T(8,128)(2,1)}), bf16[2,8,1,256,512]{4,3,0,2,1:T(8,128)(2,1)}, u32[]{:S(2)}, u32[]{:S(2)}) %all-to-all-start.1) | async-done | bytes 4194336 | tf_op jit(solution)/shard_map/all_to_all | solution.py:116
  234.7 3.9 %fusion.48 = (bf16[1,8,1,256,512]{4,3,0,2,1:T(8,128)(2,1)S(1)}, bf16[1,8,1,256,512]{4,3,0,2,1:T(8,128)(2,1)}) fusion(bf16[2,8,1,256,512]{4,3,0,2,1:T(8,128)(2,1)} %all-to-all-done.1), kind=kLoop, calls=%fused_computation.74 | loop fusion | bytes 8388608 | tf_op jit(solution)/shard_map/slice | solution.py:119
  238.6 4.0 %reshape.229 = bf16[2048,4,128]{2,1,0:T(4,128)(2,1)} reshape(bf16[1,8,1,256,512]{4,3,0,2,1:T(8,128)(2,1)} %get-tuple-element.13) | data formatting | bytes 4194304 | tf_op jit(solution)/shard_map/reshape.40
  242.6 2.0 reshape.227
  244.6 2.5 fusion.49
  247.1 0.2 fusion.21
  247.3 0.0 copy-done
  247.3 0.4 fusion.16
  247.8 0.7 maximum_bitcast_fusion
  248.4 4.6 %copy.72 = bf16[2,8,1,256,512]{4,3,1,0,2:T(8,128)(2,1)} copy(bf16[2,8,1,256,512]{4,3,0,2,1:T(8,128)(2,1)} %all-to-all-done.1) | data formatting | bytes 8388608 | tf_op jit(solution)/shard_map/all_to_all | solution.py:116
  (17 shorter events, 0.1 us)
Async XLA Ops:
  8.1 10.3 %copy-start.4 = (s32[8]{0:T(128)S(1)}, s32[8]{0:T(128)}, u32[]{:S(2)}) copy-start(s32[8]{0:T(128)} %param.15) | copy-start | bytes 100
  27.4 7.4 %copy-start.5 = (s32[8]{0:T(128)S(1)}, s32[8]{0:T(128)}, u32[]{:S(2)}) copy-start(s32[8]{0:T(128)} %param.14) | copy-start | bytes 100
  27.4 100.7 %all-to-all-start = ((bf16[2,1,8,256,512]{4,3,0,1,2:T(8,128)(2,1)}), bf16[2,1,8,256,512]{4,3,0,1,2:T(8,128)(2,1)}, u32[]{:S(2)}, u32[]{:S(2)}) async-start(bf16[2,1,8,256,512]{4,3,0,1,2:T(8,128)(2,1)} %copy.65), calls=%async_computation | async-start | bytes 8388608 | tf_op jit(solution)/shard_map/all_to_all | solution.py:114
  137.6 97.1 %all-to-all-start.1 = ((bf16[2,8,1,256,512]{4,3,0,2,1:T(8,128)(2,1)}), bf16[2,8,1,256,512]{4,3,0,2,1:T(8,128)(2,1)}, u32[]{:S(2)}, u32[]{:S(2)}) async-start(bf16[2,8,1,256,512]{4,3,0,2,1:T(8,128)(2,1)} %bitcast.78), calls=%async_computation.1 | async-start | bytes 8388608 | tf_op jit(solution)/shard_map/all_to_all | solution.py:116
  150.9 4.0 %copy-start.3 = (s32[2]{0:T(128)S(1)}, s32[2]{0:T(128)}, u32[]{:S(2)}) copy-start(s32[2]{0:T(128)} %param.11) | copy-start | bytes 28
  150.9 4.1 %copy-start.1 = (bf16[1,3,4096]{2,1,0:T(4,128)(2,1)S(1)}, bf16[1,3,4096]{2,1,0:T(4,128)(2,1)}, u32[]{:S(2)}) copy-start(bf16[1,3,4096]{2,1,0:T(4,128)(2,1)} %param.8) | copy-start | bytes 73732
  151.0 4.1 %copy-start.2 = (bf16[2,1,3,512]{3,0,2,1:T(2,128)(2,1)S(1)}, bf16[2,1,3,512]{3,0,2,1:T(2,128)(2,1)}, u32[]{:S(2)}) copy-start(bf16[2,1,3,512]{3,0,2,1:T(2,128)(2,1)} %param.10) | copy-start | bytes 18436
  244.6 2.7 %copy-start = (bf16[2048,4,128]{2,1,0:T(4,128)(2,1)S(1)}, bf16[2048,4,128]{2,1,0:T(4,128)(2,1)}, u32[]{:S(2)}) copy-start(bf16[2048,4,128]{2,1,0:T(4,128)(2,1)} %reshape.229) | copy-start | bytes 6291460
where the time goes:
time: 254 us; the launch traced here: 253 us
  waiting for transfers between devices  168 us (66%)
  local copies, waits for them, and re-layouts  57.6 us (23%)
  starting transfers between devices  11.9 us (5%)
  other arithmetic  8.73 us (3%)
  matrix products  5.91 us (2%)
    all_to_all x1, waiting for transfers between devices, on_device(): lax.all_to_all(split_kv, 'wide', split_axis=2, concat_axis=1, tiled=True)  92.5 us
    all_to_all x1, waiting for transfers between devices, on_device(): lax.all_to_all(ordered, 'wide', split_axis=1, concat_axis=3, tiled=True)  75.6 us
    mul x3, local copies, waits for them, and re-layouts, dequantize(): widened * scales.astype(jnp.float32)[..., None]  17 us
    all_to_all x1, starting transfers between devices, on_device(): lax.all_to_all(split_kv, 'wide', split_axis=2, concat_axis=1, tiled=True)  7.38 us
    unnamed x16, local copies, waits for them, and re-layouts  7.02 us
    another operation x2, local copies, waits for them, and re-layouts  5.98 us
    select_n x1, other arithmetic, on_device(): jnp.where(keeping[None, :, :, None], local_kv, jnp.zeros((), jnp.bfloat16))  5.24 us
  transfers between devices with their start and end apart: 2, of which 2 were waited for; matrix products, arithmetic and copies ran while one was open for 7% of the time, Pallas kernels for 0%

commit v1 on v0

--- a/solution.py
+++ b/solution.py
@@ -1,8 +1,11 @@
+import functools
 import math
 
 import jax
 import jax.numpy as jnp
 from jax import lax
+from jax.experimental import pallas as pl
+from jax.experimental.pallas import tpu as pltpu
 from jax.sharding import PartitionSpec as P
 
 HD = 128
@@ -79,6 +82,239 @@
     return (summed / total[..., None]).reshape(rows_count, -1).astype(jnp.bfloat16)
 
 
+import numpy as np
+
+LANES = 128
+DELAY = 4
+SLOTS = 16
+STEP_CHOICES = (128, 160, 192, 224)
+SPLITS = (0.0, 0.25, 0.5)
+
+
+def ring_position(index, n):
+    odd = index % 2
+    return (1 - odd) * (index // 2) + odd * (n - 1 - index // 2)
+
+
+def ring_device(position, n):
+    far = position // (n // 2)
+    return (1 - far) * (2 * position) + far * (2 * (n - 1 - position) + 1)
+
+
+def plan_routes(new_group, new_pages):
+    n = new_group.shape[0]
+    nodes = jnp.arange(n, dtype=jnp.int32)
+    order = np.array([ring_device(p, n) for p in range(n)])
+    groups = new_group[order]
+    pages = new_pages[order]
+    hops_forward = (ring_position(groups, n) - nodes) % n
+    hops_backward = (n - hops_forward) % n
+    count = len(SPLITS) ** n
+    digits = (np.arange(count)[:, None] // len(SPLITS) ** np.arange(n)[None, :]) % len(SPLITS)
+    eighths = jnp.asarray((np.array(SPLITS) * 8)[digits].astype(np.int32))
+    longer = (pages[None, :] * eighths) // 8
+    shorter = pages[None, :] - longer
+    short_forward = hops_forward[None, :] <= n // 2
+    moving = (hops_forward > 0)[None, :]
+    forward = jnp.where(moving, jnp.where(short_forward, shorter, longer), 0)
+    backward = jnp.where(moving, jnp.where(short_forward, longer, shorter), 0)
+    crossed_forward = ((nodes[None, :] - nodes[:, None]) % n) < hops_forward[:, None]
+    crossed_backward = ((nodes[:, None] - nodes[None, :]) % n) < hops_backward[:, None]
+    load_forward = jnp.dot(
+        forward.astype(jnp.float32), crossed_forward.astype(jnp.float32), precision="highest"
+    )
+    load_backward = jnp.dot(
+        backward.astype(jnp.float32), crossed_backward.astype(jnp.float32), precision="highest"
+    )
+    ends_forward = load_forward + jnp.where(forward > 0, (hops_forward - 1) * DELAY, 0)
+    ends_backward = load_backward + jnp.where(backward > 0, (hops_backward - 1) * DELAY, 0)
+    needed = jnp.max(jnp.maximum(ends_forward, ends_backward), axis=1).astype(jnp.int32)
+    best = jnp.argmin(needed)
+    steps = needed[best]
+    forward, backward = forward[best], backward[best]
+    mirror = (-np.arange(n)) % n
+    limits = jnp.stack([forward, backward[mirror]])
+    hops = jnp.stack([hops_forward, hops_backward[mirror]])
+    firsts = jnp.stack([jnp.zeros((n,), jnp.int32), forward[mirror]])
+    table = jnp.stack([limits, hops, firsts])
+    table = jnp.pad(jnp.tile(table, (1, 1, LANES // n)), ((0, 0), (0, 6), (0, 0)))
+    return steps, table
+
+
+def handoff_kernel(
+    n, steps, local_ref, table_ref, prefill_ref, scale_ref, out_ref,
+    own, held, staged, hist, found, found_smem, send_sem, recv_sem, copy_sem,
+):
+    index = lax.axis_index("wide")
+    place = ring_position(index, n)
+    targets = (
+        ring_device((place + 1) % n, n),
+        ring_device((place + n - 1) % n, n),
+    )
+    barrier = pltpu.get_barrier_semaphore()
+    for target in targets:
+        pl.semaphore_signal(
+            barrier, inc=1, device_id={"wide": target}, device_id_type=pl.DeviceIdType.MESH
+        )
+    pl.semaphore_wait(barrier, 2)
+
+    pages = own.shape[0]
+    width = prefill_ref.shape[-1]
+    heads = width // HD
+
+    def widen(page, carry):
+        rows = pl.ds(pl.multiple_of(page * PAGE, PAGE), PAGE)
+        for c in range(2):
+            scale = scale_ref[c, 0, rows, :].astype(jnp.float32)
+            values = prefill_ref[c, 0, rows, :].astype(jnp.float32)
+            for h in range(heads):
+                own[page, c, :, h * HD : (h + 1) * HD] = (
+                    values[:, h * HD : (h + 1) * HD] * scale[:, h : h + 1]
+                ).astype(jnp.bfloat16)
+        return carry
+
+    lax.fori_loop(0, pages, widen, 0)
+
+    sublane = lax.broadcasted_iota(jnp.int32, (8, LANES), 0)
+    lane = lax.broadcasted_iota(jnp.int32, (8, LANES), 1)
+    mirrored = (n - place) % n
+    here = ((sublane == 0) & (lane == place)) | ((sublane == 1) & (lane == mirrored))
+    limits = table_ref[0]
+    hops = table_ref[1]
+    firsts = table_ref[2]
+
+    def arrivals(step, seen, to_go, page):
+        landed = jnp.where(here & (to_go == 1), page + 1, 0)
+        landed = jnp.sum(landed, axis=1, keepdims=True)
+        return jnp.where(lane == landed - 1, step - DELAY, seen)
+
+    def advance(step, sent, seen, first):
+        if first:
+            to_go = jnp.zeros((8, LANES), jnp.int32)
+            page = to_go
+        else:
+            past = hist[step % DELAY]
+            past = pltpu.roll(past, 1, 1)
+            to_go = past % 16
+            page = past // 16
+            seen = arrivals(step, seen, to_go, page)
+        forwards = to_go > 1
+        injects = jnp.logical_not(forwards) & (sent < limits)
+        now = jnp.where(forwards, page * 16 + to_go - 1, jnp.where(injects, (firsts + sent) * 16 + hops, 0))
+        hist[step % DELAY] = now
+        code = jnp.where(here, jnp.where(forwards, pages, jnp.where(injects, firsts + sent, 0)), 0)
+        codes = (
+            jnp.sum(jnp.where(sublane == 0, code, 0)),
+            jnp.sum(jnp.where(sublane == 1, code, 0)),
+        )
+        return sent + injects.astype(jnp.int32), seen, codes
+
+    def hop(step, way):
+        return pltpu.make_async_remote_copy(
+            src_ref=staged.at[way, step % SLOTS],
+            dst_ref=held.at[way, step],
+            send_sem=send_sem.at[way, step % SLOTS],
+            recv_sem=recv_sem.at[way, step % SLOTS],
+            device_id={"wide": targets[way]},
+            device_id_type=pl.DeviceIdType.MESH,
+        )
+
+    def one_step(step, carry, first, reuse):
+        sent, seen = carry
+        sent, seen, codes = advance(step, sent, seen, first)
+        for way in range(2):
+            if reuse:
+                hop(step - SLOTS, way).wait_send()
+            mine = own[jnp.minimum(codes[way], pages - 1)]
+            if not first:
+                hop(step - DELAY, way).wait_recv()
+                mine = jnp.where(codes[way] >= pages, held[way, step - DELAY], mine)
+            staged[way, step % SLOTS] = mine
+            hop(step, way).start()
+        return sent, seen
+
+    carry = (jnp.zeros((8, LANES), jnp.int32), jnp.full((8, LANES), -1, jnp.int32))
+    carry = lax.fori_loop(0, DELAY, lambda t, c: one_step(t, c, True, False), carry)
+    carry = lax.fori_loop(DELAY, SLOTS, lambda t, c: one_step(t, c, False, False), carry)
+    carry = lax.fori_loop(SLOTS, steps, lambda t, c: one_step(t, c, False, True), carry)
+    sent, seen = carry
+
+    def settle(step, seen):
+        past = pltpu.roll(hist[step % DELAY], 1, 1)
+        for way in range(2):
+            hop(step - DELAY, way).wait_recv()
+        return arrivals(step, seen, past % 16, past // 16)
+
+    seen = lax.fori_loop(steps, steps + DELAY, settle, seen)
+
+    def drain(step, carry):
+        for way in range(2):
+            hop(step, way).wait_send()
+        return carry
+
+    lax.fori_loop(steps - SLOTS, steps, drain, 0)
+
+    found[...] = seen
+    fetch = pltpu.make_async_copy(found, found_smem, copy_sem)
+    fetch.start()
+    fetch.wait()
+
+    stays = local_ref[0]
+    length = local_ref[1]
+
+    def place_page(page, carry):
+        forward = found_smem[0, page]
+        backward = found_smem[1, page]
+        from_backward = (backward >= 0).astype(jnp.int32)
+        at = jnp.where(from_backward == 1, backward, jnp.maximum(forward, 0))
+        rows = pl.ds(pl.multiple_of(page * PAGE, PAGE), PAGE)
+        block = jnp.where(stays == 1, own[page], held[from_backward, at])
+        block = jnp.where(page < length, block, jnp.zeros_like(block))
+        for c in range(2):
+            out_ref[c, 0, 0, rows, :] = block[c]
+        return carry
+
+    lax.fori_loop(0, pages, place_page, 0)
+
+
+def handoff(steps, collective_id, n, local, table, prefill, prefill_scale):
+    prompt_len, width = prefill.shape[2:]
+    pages = prompt_len // PAGE
+    return pl.pallas_call(
+        functools.partial(handoff_kernel, n, steps),
+        out_shape=jax.ShapeDtypeStruct((2, 1, 1, prompt_len, width), jnp.bfloat16),
+        in_specs=[pl.BlockSpec(memory_space=pltpu.SMEM)]
+        + [pl.BlockSpec(memory_space=pltpu.VMEM)] * 3,
+        out_specs=pl.BlockSpec(memory_space=pltpu.VMEM),
+        scratch_shapes=[
+            pltpu.VMEM((pages, 2, PAGE, width), jnp.bfloat16),
+            pltpu.VMEM((2, steps, 2, PAGE, width), jnp.bfloat16),
+            pltpu.VMEM((2, SLOTS, 2, PAGE, width), jnp.bfloat16),
+            pltpu.VMEM((DELAY, 8, LANES), jnp.int32),
+            pltpu.VMEM((8, LANES), jnp.int32),
+            pltpu.SMEM((8, LANES), jnp.int32),
+            pltpu.SemaphoreType.DMA((2, SLOTS)),
+            pltpu.SemaphoreType.DMA((2, SLOTS)),
+            pltpu.SemaphoreType.DMA,
+        ],
+        compiler_params=pltpu.CompilerParams(
+            collective_id=collective_id, has_side_effects=True, vmem_limit_bytes=50 * 2**20
+        ),
+    )(local, table, prefill, prefill_scale)
+
+
+def exchange(prefill, prefill_scale, own_len, arrival, groups_count, per_group):
+    prompt_len, width_here = prefill.shape[2:]
+    positions = jnp.arange(prompt_len, dtype=jnp.int32)
+    local_kv = dequantize(prefill, prefill_scale)
+    keeping = positions[None, :] < own_len[:, None]
+    local_kv = jnp.where(keeping[None, :, :, None], local_kv, jnp.zeros((), jnp.bfloat16))
+    split_kv = local_kv.reshape(2, per_group, groups_count, prompt_len // groups_count, width_here)
+    held = lax.all_to_all(split_kv, "wide", split_axis=2, concat_axis=1, tiled=True)
+    ordered = held[:, arrival]
+    return lax.all_to_all(ordered, "wide", split_axis=1, concat_axis=3, tiled=True)
+
+
 def on_device(queries, cache_kv, fresh_kv, ctx_len, prefill, prefill_scale, new_group, new_pages):
     groups_count = lax.axis_size("wide")
     device_index = lax.axis_index("wide")
@@ -86,8 +322,6 @@
     per_group = new_total // groups_count
     resident_count = cache_kv.shape[1]
     prompt_len = prefill.shape[2]
-    piece_len = prompt_len // groups_count
-    width_here = prefill.shape[3]
     slot_ids = new_group * per_group + group_ranks(new_group)
     arrival = (
         jnp.zeros((new_total,), jnp.int32).at[slot_ids].set(jnp.arange(new_total, dtype=jnp.int32))
@@ -95,7 +329,7 @@
     new_len = new_pages * PAGE
     first_slot = device_index * per_group
     slot_len = lax.dynamic_slice_in_dim(new_len[arrival], first_slot, per_group)
-    positions = jnp.arange(prompt_len, dtype=jnp.int32)
+    own_len = lax.dynamic_slice_in_dim(new_len, first_slot, per_group)
     asked_rows = queries[0]
     own_fresh = fresh_kv[:, 0]
     older_rows = attend(
@@ -106,14 +340,30 @@
         own_fresh[0, :resident_count],
         own_fresh[1, :resident_count],
     )
-    own_len = lax.dynamic_slice_in_dim(new_len, first_slot, per_group)
-    local_kv = dequantize(prefill, prefill_scale)
-    keeping = positions[None, :] < own_len[:, None]
-    local_kv = jnp.where(keeping[None, :, :, None], local_kv, jnp.zeros((), jnp.bfloat16))
-    split_kv = local_kv.reshape(2, per_group, groups_count, piece_len, width_here)
-    held = lax.all_to_all(split_kv, "wide", split_axis=2, concat_axis=1, tiled=True)
-    ordered = held[:, arrival]
-    handed = lax.all_to_all(ordered, "wide", split_axis=1, concat_axis=3, tiled=True)
+
+    def by_pieces():
+        return exchange(prefill, prefill_scale, own_len, arrival, groups_count, per_group)
+
+    if groups_count == 8 and per_group == 1 and prompt_len == LANES * PAGE:
+        steps, table = plan_routes(new_group, new_pages)
+        parts_count = lax.axis_size("parts")
+        for shift in range(1, parts_count):
+            steps = jnp.maximum(
+                steps,
+                lax.ppermute(
+                    steps, "parts", [(p, (p + shift) % parts_count) for p in range(parts_count)]
+                ),
+            )
+        source = lax.dynamic_index_in_dim(arrival, device_index, keepdims=False)
+        local = jnp.stack([(source == device_index).astype(jnp.int32), slot_len[0] // PAGE])
+        choice = sum((steps > limit).astype(jnp.int32) for limit in STEP_CHOICES)
+        branches = [
+            functools.partial(handoff, limit, 1 + i, groups_count, local, table, prefill, prefill_scale)
+            for i, limit in enumerate(STEP_CHOICES)
+        ]
+        handed = lax.switch(choice, branches + [by_pieces])
+    else:
+        handed = by_pieces()
     newer_rows = attend(
         asked_rows[resident_count:],
         handed[0, 0],

time: 254 us -> 208 us (0.82)
  waiting for transfers between devices: 168 us -> 0.01 us
  Pallas kernels: 0 us -> 149 us
  local copies, waits for them, and re-layouts: 57.6 us -> 35.7 us
  starting transfers between devices: 11.9 us -> 2.97 us
  between operations: 0.81 us -> 7.36 us
  matrix products: 5.91 us -> 3.35 us
    all_to_all x2 -> x0, waiting for transfers between devices: 168 us -> none  [the longest x1 92.5 us: on_device(): lax.all_to_all(split_kv, 'wide', split_axis=2, concat_axis=1, tiled=True)]
    pallas_call x0 -> x1, Pallas kernels: none -> 149 us  [handoff(): pl.pallas_call(functools.partial(handoff_kernel, n, steps), out_shape=jax...]
    mul x3 -> x0, local copies, waits for them, and re-layouts: 17 us -> none  [dequantize(): widened * scales.astype(jnp.float32)[..., None]]
    all_to_all x2 -> x0, starting transfers between devices: 11.9 us -> none  [the longest x1 7.38 us: on_device(): lax.all_to_all(split_kv, 'wide', split_axis=2, concat_axis=1, tiled=True)]
    unnamed x16 -> x13, local copies, waits for them, and re-layouts: 7.02 us -> 17.1 us
    all_to_all x2 -> x0, local copies, waits for them, and re-layouts: 9.14 us -> none  [the longest x1 4.57 us: on_device(): lax.all_to_all(split_kv, 'wide', split_axis=2, concat_axis=1, tiled=True)]
    another operation x2 -> x4, local copies, waits for them, and re-layouts: 5.98 us -> 0.62 us
    select_n x2, other arithmetic: 5.24 us -> 1.19 us  [the longest x1 1.17 us: plan_routes(): backward = jnp.where(moving, jnp.where(short_forward, longer, shorter), 0)]
  transfers between devices with their start and end apart: 2 -> 1, of which waited for: 2 -> 0; matrix products, arithmetic and copies ran while one was open for 7% -> 10% of each run, Pallas kernels for 0% -> 0%
where the time goes in v1:
time: 208 us; the launch traced here: 207 us
  Pallas kernels  149 us (72%)
  local copies, waits for them, and re-layouts  35.7 us (17%)
  other arithmetic  8.81 us (4%)
  between operations  7.36 us (4%)
  matrix products  3.35 us (2%)
  starting transfers between devices  2.97 us (1%)
    pallas_call x1, Pallas kernels, handoff(): pl.pallas_call(functools.partial(handoff_kernel, n, steps), out_shape=jax...  149 us
    unnamed x13, local copies, waits for them, and re-layouts  17.1 us
    slice x1, local copies, waits for them, and re-layouts, on_device(): cache_kv[0]  4.54 us
    slice x1, local copies, waits for them, and re-layouts, on_device(): handed[0, 0]  4.51 us
  transfers between devices with their start and end apart: 1, of which 0 were waited for; matrix products, arithmetic and copies ran while one was open for 10% of the time, Pallas kernels for 0%

profile of v1, /device:TPU:0, one launch (start us, length us, event | category | flops | bytes accessed | tf_op | source)
XLA Modules:
  0.0 207.1 jit_solution(12949084611992132113)
XLA Ops:
  0.7 0.7 pad_clamp_fusion.2
  1.3 0.9 convert_reduce_fusion
  2.2 1.3 gather_fusion.2
  3.5 0.7 compare_select_fusion.2
  4.2 0.6 scatter_custom_fusion
  4.9 1.3 gather_fusion.3
  6.2 1.2 fusion.17
  7.3 0.4 convolution_add_fusion.1
  7.7 0.4 fusion.5
  8.1 0.7 iota_reduce_fusion
  10.7 0.6 dynamic_slice.20
  11.3 3.0 %collective-permute-start = (s32[]{:T(128)}, s32[]{:T(128)}, u32[]{:S(2)}, u32[]{:S(2)}) collective-permute-start(s32[]{:T(128)} %bitcast.21), channel_id=1, source_target_pairs={{0,16},{16,0},{1,17},{17,1},{2,18},{18,2},{3,19},{19,3},{4,20},{20... | collective-permute-start | bytes 20 | tf_op jit(solution)/shard_map/ppermute | solution.py:353
  14.3 0.2 dynamic-slice_reduce_fusion
  14.5 0.2 fusion.81
  14.7 0.7 broadcast_multiply_fusion
  15.4 0.6 gather_fusion.1
  16.0 0.6 dynamic_slice.19
  18.5 0.7 dynamic_slice.23
  19.2 0.7 iota_compare_fusion.1
  19.9 0.8 slice_reduce_fusion
  20.7 0.8 slice_bitcast_fusion
  21.5 0.7 slice_convert_fusion.1
  22.2 0.7 slice_convert_fusion
  22.8 0.7 pad_clamp_fusion.1
  23.5 0.6 gather_fusion.5
  24.1 0.6 gather_fusion.4
  24.8 0.1 copy.121
  24.9 0.6 gather_fusion.6
  26.9 0.1 fusion.37
  27.1 4.5 %fusion.82 = (bf16[1,2,1024,512]{3,2,1,0:T(8,128)(2,1)}, bf16[1,2,1024,512]{3,2,1,0:T(8,128)(2,1)}) fusion(bf16[2,2,1024,512]{3,2,1,0:T(8,128)(2,1)} %param.22), kind=kLoop, calls=%fused_computation.167 | loop fusion | bytes 8388608 | tf_op jit(solution)/shard_map/slice | solution.py:337
  31.6 3.0 %copy.141 = bf16[1,2,1024,512]{2,3,1,0:T(8,128)(2,1)S(1)} copy(bf16[1,2,1024,512]{3,2,1,0:T(8,128)(2,1)} %get-tuple-element.227) | data formatting | bytes 4194304
  34.6 0.1 fusion.32
  34.8 0.5 fusion.85
  35.2 0.2 fusion.11
  35.5 3.0 %copy.142 = bf16[1,2,1024,512]{2,3,1,0:T(8,128)(2,1)S(1)} copy(bf16[1,2,1024,512]{3,2,1,0:T(8,128)(2,1)} %get-tuple-element.228) | data formatting | bytes 4194304
  38.5 0.7 fusion.9
  40.6 149.5 %conditional.1 = (bf16[2,1,1,2048,512]{4,3,0,2,1:T(8,128)(2,1)}) conditional(s32[]{:T(128)} %clamp.3, (s32[3,2,8]{2,1,0:T(2,128)S(1)}, s32[2]{0:T(128)S(1)}, bf16[2,1,2048,512]{3,2,1,0:T(8,128)(2,1)}, bf16[2,1,2048,4]{2,3,1,0:T(4,128)(2,1)S(1)}) %tuple.81, (s32[3,2,8]{2,1,0:T(2,128)S(1)}, s32[2]{0:T(128)S(1)}, ...), branch_computations={%region_6.7_spmd, %region_7.8_spmd, %region_8.9_spmd, %region_9.10... | conditional | flops 8408088 | bytes 96706744 | solution.py:364
  40.6 0.5 copy.123.scale_ref
  41.2 0.1 tile.20
  41.3 148.9 %branch_1_fun.1 = bf16[2,1,1,2048,512]{4,3,2,1,0:T(8,128)(2,1)} custom-call(s32[2]{0:T(128)S(1)} %get-tuple-element.66.local_ref, s32[3,8,128]{2,1,0:T(8,128)S(1)} %pad.12.table_ref, bf16[2,1,2048,512]{3,2,1,0:T(8,128)(2,1)} %get-tuple-element.68.prefill_ref, bf16[2,1,2048,4]{3,2,1,0:T(8,128)(2,1)S(1)} %copy.123.scale_ref), custom_call_target="tpu_custom_call" | custom-call | tf_op jit(solution)/shard_map/cond/branch_1_fun/pallas_call | solution.py:283
  190.2 4.5 %fusion.83 = (bf16[1,1,1,2048,512]{4,3,0,2,1:T(8,128)(2,1)}, bf16[1,1,1,2048,512]{4,3,0,2,1:T(8,128)(2,1)}) fusion(bf16[2,1,1,2048,512]{4,3,0,2,1:T(8,128)(2,1)} %get-tuple-element.248), kind=kLoop, calls=%fused_computation.168 | loop fusion | bytes 8388608 | tf_op jit(solution)/shard_map/slice | solution.py:369
  194.7 2.9 %copy.143 = bf16[1,1,1,2048,512]{3,4,2,1,0:T(8,128)(2,1)S(1)} copy(bf16[1,1,1,2048,512]{4,3,0,2,1:T(8,128)(2,1)} %get-tuple-element.229) | data formatting | bytes 4194304
  197.6 0.5 fusion.84
  198.1 0.2 fusion.13
  198.3 2.9 %copy.144 = bf16[1,1,1,2048,512]{3,4,2,1,0:T(8,128)(2,1)S(1)} copy(bf16[1,1,1,2048,512]{4,3,0,2,1:T(8,128)(2,1)} %get-tuple-element.230) | data formatting | bytes 4194304
  201.3 0.7 fusion.10
  202.0 0.7 maximum_bitcast_fusion
  202.6 4.5 %copy.167 = bf16[2,1,1,2048,512]{4,3,2,1,0:T(8,128)(2,1)} copy(bf16[2,1,1,2048,512]{4,3,2,1,0:T(8,128)(2,1)} %bitcast.115) | data formatting | bytes 8388608
  (30 shorter events, 0.4 us)
Async XLA Ops:
  0.6 26.3 %copy-start.1 = (bf16[2,1,3,512]{3,0,2,1:T(2,128)(2,1)S(1)}, bf16[2,1,3,512]{3,0,2,1:T(2,128)(2,1)}, u32[]{:S(2)}) copy-start(bf16[2,1,3,512]{3,0,2,1:T(2,128)(2,1)} %param.23) | copy-start | bytes 18436
  0.6 26.4 %copy-start.2 = (s32[2]{0:T(128)S(1)}, s32[2]{0:T(128)}, u32[]{:S(2)}) copy-start(s32[2]{0:T(128)} %param.24) | copy-start | bytes 28
  11.3 28.0 %collective-permute-start = (s32[]{:T(128)}, s32[]{:T(128)}, u32[]{:S(2)}, u32[]{:S(2)}) collective-permute-start(s32[]{:T(128)} %bitcast.21), channel_id=1, source_target_pairs={{0,16},{16,0},{1,17},{17,1},{2,18},{18,2},{3,19},{19,3},{4,20},{20... | collective-permute-start | bytes 20 | tf_op jit(solution)/shard_map/ppermute | solution.py:353
  34.7 5.9 %copy-start = (bf16[2,1,2048,4]{2,3,1,0:T(4,128)(2,1)S(1)}, bf16[2,1,2048,4]{2,3,1,0:T(4,128)(2,1)}, u32[]{:S(2)}) copy-start(bf16[2,1,2048,4]{2,3,1,0:T(4,128)(2,1)} %param.26) | copy-start | bytes 98308
